TPU v7x, 128 devices: a whole 4x4x4 slice. The times are simulated.
128 devices in a mesh: pass: 64 (over x_hi, z, y, core), qry: 2 (over x_lo).
Axes of the slice: x: 4 (x_hi: 2, x_lo: 2; x = x_hi * 2 + x_lo), y: 4, z: 4, core: 2. Of those that a mesh axis runs over, the one named last changes fastest.
Arguments:
- student_queries: bfloat16 [4096, 768], P('qry'), may hold values from -8 to 8
- teacher_queries: bfloat16 [4096, 1024], P('qry'), may hold values from -8 to 8
- student_passages: bfloat16 [65536, 768], P('pass'), may hold values from -8 to 8
- teacher_passages: bfloat16 [65536, 1024], P('pass'), may hold values from -8 to 8
- positives: int32 [4096], P('qry'), may hold values from 0 to 65535
Outputs:
- loss: float32 [], replicated
- grad_queries: float32 [4096, 768], P('qry')
- grad_passages: float32 [65536, 768], P(('pass', 'qry'))
All inputs are finite; a program needn't handle non-finite values.
Results may differ from a plain program's by a relative error of at most 0.0026.
Values sent between devices are 32-bit elements; how exact they have to be, the bound alone decides.
A program may use at most 128 MiB of HBM per device.

v0:
```python
import math

import jax
import jax.numpy as jnp
from jax import lax
from jax.sharding import PartitionSpec as P

LOGIT_GAIN = 3.0
CE_WEIGHT = 0.5


def shards(student_queries, teacher_queries, student_passages, teacher_passages, positives):
    query_rows = student_queries.shape[0]
    passage_rows = student_passages.shape[0]
    student_scale = LOGIT_GAIN / math.sqrt(student_queries.shape[1])
    teacher_scale = LOGIT_GAIN / math.sqrt(teacher_queries.shape[1])
    all_queries = query_rows * lax.axis_size("qry")
    all_passages = passage_rows * lax.axis_size("pass")
    contract_last = (((1,), (1,)), ((), ()))
    student_logits = (
        lax.dot_general(
            student_queries, student_passages, contract_last, preferred_element_type=jnp.float32
        )
        * student_scale
    )
    teacher_logits = (
        lax.dot_general(
            teacher_queries, teacher_passages, contract_last, preferred_element_type=jnp.float32
        )
        * teacher_scale
    )
    first_column = lax.axis_index("pass") * passage_rows
    columns = first_column + lax.broadcasted_iota(jnp.int32, (1, passage_rows), 1)
    is_positive = columns == positives[:, None]
    local_positive = jnp.sum(jnp.where(is_positive, student_logits, 0.0), axis=1)
    student_peak, teacher_peak = lax.pmax(
        (jnp.max(student_logits, axis=1), jnp.max(teacher_logits, axis=1)), "pass"
    )
    teacher_weights = jnp.exp(teacher_logits - teacher_peak[:, None])
    student_total, teacher_total, cross_total, positive_logit = lax.psum(
        (
            jnp.sum(jnp.exp(student_logits - student_peak[:, None]), axis=1),
            jnp.sum(teacher_weights, axis=1),
            jnp.sum(teacher_weights * (teacher_logits - student_logits), axis=1),
            local_positive,
        ),
        "pass",
    )
    student_lse = student_peak + jnp.log(student_total)
    teacher_lse = teacher_peak + jnp.log(teacher_total)
    cross = cross_total / teacher_total
    row_loss = cross - teacher_lse + student_lse + CE_WEIGHT * (student_lse - positive_logit)
    loss = lax.psum(jnp.sum(row_loss), "qry") / all_queries
    student_probs = jnp.exp(student_logits - student_lse[:, None])
    teacher_probs = jnp.exp(teacher_logits - teacher_lse[:, None])
    logit_grads = (
        (1.0 + CE_WEIGHT) * student_probs
        - teacher_probs
        - CE_WEIGHT * is_positive.astype(jnp.float32)
    ).astype(jnp.bfloat16)
    local_grads = (
        jnp.dot(logit_grads, student_passages, preferred_element_type=jnp.float32) * student_scale
    )
    query_grads = lax.psum(local_grads, "pass")
    passage_terms = (
        lax.dot_general(
            logit_grads,
            student_queries,
            (((0,), (0,)), ((), ())),
            preferred_element_type=jnp.float32,
        )
        * student_scale
    )
    passage_share = lax.psum_scatter(passage_terms, "qry", scatter_dimension=0, tiled=True)
    return (loss, query_grads, passage_share * all_passages)


def solution(mesh):
    return jax.shard_map(
        shards,
        mesh=mesh,
        in_specs=(P("qry", None), P("qry", None), P("pass", None), P("pass", None), P("qry")),
        out_specs=(P(), P("qry", None), P(("pass", "qry"), None)),
        check_vma=False,
    )
```

profile of v0, /device:TPU:1, one launch (start us, length us, event | category | flops | bytes accessed | tf_op | source)
XLA Modules:
  0.0 1407.2 jit_solution(1208290566909770370)
XLA Ops:
  8.0 0.0 copy-start
  8.0 0.0 reduce-scatter.2.cloned.1.call-start
  8.1 0.0 copy-start.2
  8.1 10.8 multiply_reduce_fusion.1
  18.8 167.0 %pmax.14 = f32[2048]{0:T(1024)S(1)} all-reduce(f32[2048]{0:T(1024)S(1)} %get-tuple-element.14), channel_id=1, replica_groups=mesh['pass'=64,'qry'=2] {'pass'}, use_global_device_ids=true, to_apply=%region_1.2 | all-reduce | flops 2048 | bytes 16384 | tf_op jit(solution)/shard_map/pmax | solution.py:36
  185.8 0.0 copy-done
  185.8 0.0 copy-done.2
  185.8 10.5 multiply_reduce_fusion
  196.4 171.3 %pmax.15 = f32[2048]{0:T(1024)S(1)} all-reduce(f32[2048]{0:T(1024)S(1)} %get-tuple-element.5), channel_id=1, replica_groups=mesh['pass'=64,'qry'=2] {'pass'}, use_global_device_ids=true, to_apply=%region_7.8 | all-reduce | flops 2048 | bytes 16384 | tf_op jit(solution)/shard_map/pmax | solution.py:36
  367.7 4.8 exponential_reduce_fusion
  372.5 315.9 %all-reduce = (f32[2048]{0:T(1024)S(1)}, f32[2048]{0:T(1024)S(1)}, f32[2048]{0:T(1024)S(1)}, f32[2048]{0:T(1024)S(1)}) all-reduce(f32[2048]{0:T(1024)S(1)} %exponential_reduce_fusion, f32[2048]{0:T(1024)S(1)} %get-tuple-element.6, f32[2048]{0:T(1024)S(1)} %get-tuple-element.4, ...), channel_id=1, replica_groups=mesh['pass'=64,'qry'=2] {'pass'}, use_global_device_ids=true, to_apply=%region_9.10 | all-reduce | flops 8192 | bytes 65536 | tf_op jit(solution)/shard_map/psum | solution.py:40
  688.3 0.6 add_reduce_fusion
  689.0 7.9 fusion.2
  696.9 0.0 copy-start.1
  696.9 1.9 copy-done.1
  698.8 5.1 convolution_multiply_fusion.1
  703.9 0.0 reduce-scatter.2.cloned.1.call-update
  704.0 0.0 all-reduce.3.cloned.1.call-start
  704.0 8.9 convolution_multiply_fusion
  712.9 0.0 all-reduce.3.cloned.1.call-update
  712.9 4.9 psum.46
  718.5 33.5 %reduce-scatter.2.cloned.1.call-done = f32[512,768]{1,0:T(8,128)} async-done(((f32[1024,768]{1,0:T(8,128)}), f32[512,768]{1,0:T(8,128)}) %reduce-scatter.2.cloned.1.call-update) | async-done | bytes 1572880 | tf_op jit(solution)/shard_map/reduce_scatter | solution.py:74
  751.9 2.7 broadcast_multiply_fusion
  754.6 638.1 %all-reduce.3.cloned.1.call-done = f32[2048,768]{1,0:T(8,128)} async-done(((f32[2048,768]{1,0:T(8,128)}), f32[2048,768]{1,0:T(8,128)}) %all-reduce.3.cloned.1.call-update) | async-done | bytes 6291472 | tf_op jit(solution)/shard_map/psum | solution.py:64
  1392.7 5.9 copy.9
  (1 shorter events, 0.0 us)
Async XLA Ops:
  8.0 177.8 %copy-start = (bf16[2048,768]{1,0:T(8,128)(2,1)S(1)}, bf16[2048,768]{1,0:T(8,128)(2,1)}, u32[]{:S(2)}) copy-start(bf16[2048,768]{1,0:T(8,128)(2,1)} %param.5) | copy-start | bytes 9437188
  8.0 743.9 %reduce-scatter.2.cloned.1.call-start = ((), (), s32[]{:S(2)}) async-start(), calls=%async_computation.2 | async-start | bytes 4718592 | tf_op jit(solution)/shard_map/reduce_scatter | solution.py:74
  8.1 177.7 %copy-start.2 = (s32[2048]{0:T(1024)S(1)}, s32[2048]{0:T(1024)}, u32[]{:S(2)}) copy-start(s32[2048]{0:T(1024)} %param.9) | copy-start | bytes 24580
  696.9 1.9 copy-start.1
  704.0 688.7 %all-reduce.3.cloned.1.call-start = ((), (), s32[]{:S(2)}) async-start(), calls=%async_computation.1 | async-start | bytes 12582912 | tf_op jit(solution)/shard_map/psum | solution.py:64
Sparse Core Ops, SparseCore 0:
  704.1 47.8 reduce-scatter.1
Sparse Core Ops, SparseCore 1:
  713.0 679.6 all-reduce.2
where the time goes:
time: 1410 us
  waiting for transfers between devices  672 us (48%)
  blocking collectives  659 us (47%)
  matrix products  35.3 us (3%)
  between operations  17.3 us (1%)
  other arithmetic  16 us (1%)
    psum x1, waiting for transfers between devices, shards(): query_grads = lax.psum(local_grads, 'pass')  638 us
    pmax x2, blocking collectives, shards(): lax.pmax((jnp.max(student_logits, axis=1), jnp.max(teacher_logits, axis=1...  338 us
    psum x1, blocking collectives, shards(): lax.psum((jnp.sum(jnp.exp(student_logits - student_peak[:, None]), axis=1...  316 us
    reduce_scatter x1, waiting for transfers between devices, shards(): lax.psum_scatter(passage_terms, 'qry', scatter_dimension=0, tiled=True)  33.5 us
  transfers between devices with their start and end apart: 2, of which 2 were waited for; matrix products, arithmetic and copies ran while one was open for 1% of the time, Pallas kernels for 0%

commit v1 on v0

v1 whole, which is shorter than its diff:
```python
import functools
import math

import jax
import jax.numpy as jnp
from jax import lax
from jax.experimental import pallas as pl
from jax.experimental.pallas import tpu as pltpu
from jax.sharding import PartitionSpec as P

LOGIT_GAIN = 3.0
CE_WEIGHT = 0.5
LOG2E = math.log2(math.e)
LN2 = math.log(2.0)
MESH = pl.DeviceIdType.MESH
NT = (((1,), (1,)), ((), ()))
TN = (((0,), (0,)), ((), ()))
NN = (((1,), (0,)), ((), ()))
TILE = 256
CHUNK = 512
CHUNKS = 4
STATS = 8


def dot(a, b, dims):
    return lax.dot_general(a, b, dims, preferred_element_type=jnp.float32)


def aligned(x, m):
    return x if isinstance(x, int) else pl.multiple_of(x, m)


def wide(rows):
    return jnp.concatenate([rows[k : k + 1, :] for k in range(rows.shape[0])], axis=1)


def log_total(values):
    peak = functools.reduce(jnp.maximum, values)
    total = functools.reduce(jnp.add, [jnp.exp2(v - peak) for v in values])
    return peak + jnp.log(total) * LOG2E


def kernel(
    sq_hbm, tq_hbm, sp_hbm, tp_hbm, pos_ref, loss_ref, out, pas,
    sq, tq, sp, tp, es, et, stat, bs0, bt0, mx0, bs1, bt1, mx1, g, own, half, rfar, rnear, rx, ps, pr,
    sb1, s1, sb2, s2, lse, lb1, lb2, lb3, lacc, ssem, rsem, lsem,
):
    queries, ds = sq.shape
    passages, dt = tp.shape
    cs = LOGIT_GAIN / math.sqrt(ds) * LOG2E
    ct = LOGIT_GAIN / math.sqrt(dt) * LOG2E
    scale = LOGIT_GAIN / math.sqrt(ds)
    tiles = passages // TILE
    p, q = lax.axis_index("pass"), lax.axis_index("qry")
    core, y, z, xh = p % 2, (p // 2) % 4, (p // 8) % 4, p // 32

    def dev(c=core, yy=y, zz=z, x=xh, qq=q):
        return (((x * 4 + zz) * 4 + yy) * 2 + c, qq)

    loads = {}

    def load(name, src, dst):
        loads[name] = pltpu.make_async_copy(src, dst, lsem.at[len(loads)])
        loads[name].start()

    def rows(c):
        return pl.ds(c * CHUNK, CHUNK)

    load("sp", sp_hbm, sp)
    load("sq0", sq_hbm.at[rows(0)], sq.at[rows(0)])
    load("tp", tp_hbm, tp)
    load("tq0", tq_hbm.at[rows(0)], tq.at[rows(0)])
    for c in range(1, CHUNKS):
        load(f"sq{c}", sq_hbm.at[rows(c)], sq.at[rows(c)])
        load(f"tq{c}", tq_hbm.at[rows(c)], tq.at[rows(c)])

    group1 = [(a, b) for a in range(2) for b in range(4) if (a, b) != (0, 0)]
    peers1 = [dev(c=(core + a) % 2, yy=(y + b) % 4) for a, b in group1]
    peers2 = [dev(x=(xh + a) % 2, zz=(z + b) % 4) for a, b in group1]
    partner = dev(c=1 - core)
    across = dev(x=1 - xh)
    other = dev(qq=1 - q)
    barrier = pltpu.get_barrier_semaphore()
    everyone = peers1 + peers2 + [other]
    for peer in everyone:
        pl.semaphore_signal(barrier, inc=1, device_id=peer, device_id_type=MESH)

    counts = {"sem": 0}
    sent = []

    def sem():
        counts["sem"] += 1
        return counts["sem"] - 1

    def send(src, dst, peer, i=None):
        i = sem() if i is None else i
        copy = pltpu.make_async_remote_copy(
            src_ref=src, dst_ref=dst, send_sem=ssem.at[i], recv_sem=rsem.at[i], device_id=peer, device_id_type=MESH
        )
        copy.start()
        return copy

    def post(src, dst, peer):
        copy = send(src, dst, peer)
        sent.append(copy)
        return copy

    def spread(src, slots, peers, each):
        i = sem()
        for n, peer in enumerate(peers):
            send(src, each(n), peer, i)
        whole = slots.at[pl.ds(0, STATS - 1)]
        both = pltpu.make_async_remote_copy(
            src_ref=whole, dst_ref=whole, send_sem=ssem.at[i], recv_sem=rsem.at[i], device_id=peers[0], device_id_type=MESH
        )
        sent.append(both)
        return both

    buffers = ((bs0, bt0, mx0), (bs1, bt1, mx1))

    def products(i, piece):
        c, t = divmod(i, tiles)
        bs, bt, mx = buffers[i % 2]
        teacher, j = divmod(piece, 2)
        w = CHUNK // 2
        if t == 0 and j == 0:
            if c == 0:
                loads["tp" if teacher else "sp"].wait()
            loads[f"{'tq' if teacher else 'sq'}{c}"].wait()
        a = (tp if teacher else sp)[pl.ds(t * TILE, TILE), :]
        b = (tq if teacher else sq)[pl.ds(c * CHUNK + j * w, w), :]
        r = dot(a, b, NT)
        (bt if teacher else bs)[:, j * w : (j + 1) * w] = r
        mx[teacher, :, j * w : (j + 1) * w] = jnp.max(r.reshape(TILE // 8, 8, w), axis=0)

    def exponentials(i, j):
        c, t = divmod(i, tiles)
        bs, bt, mx = buffers[i % 2]
        w = CHUNK // 2
        cut = slice(j * w, (j + 1) * w)
        d = pl.ds(c * CHUNK + j * w, w)
        s2 = bs[:, cut] * cs
        t2 = bt[:, cut] * ct
        ms = jnp.max(mx[0, :, cut], axis=0, keepdims=True) * cs
        mt = jnp.max(mx[1, :, cut], axis=0, keepdims=True) * ct
        e_s = jnp.exp2(s2 - ms)
        e_t = jnp.exp2(t2 - mt)
        row = lax.broadcasted_iota(jnp.int32, (TILE, w), 0) + t * TILE
        at_positive = jnp.where(row == pos_ref[0:1, d] - p * passages, s2, 0.0)
        es[pl.ds(t * TILE, TILE), d] = e_s
        et[pl.ds(t * TILE, TILE), d] = e_t
        stat[t, 0:1, d] = ms
        stat[t, 1:2, d] = mt
        stat[t, 2:3, d] = jnp.sum(e_s, axis=0, keepdims=True)
        stat[t, 3:4, d] = jnp.sum(e_t, axis=0, keepdims=True)
        stat[t, 4:5, d] = jnp.sum(e_t * (t2 - s2), axis=0, keepdims=True)
        stat[t, 5:6, d] = jnp.sum(at_positive, axis=0, keepdims=True)

    def logits(c):
        for i in range(c * tiles, (c + 1) * tiles):
            for j in range(4):
                if i + 1 < CHUNKS * tiles:
                    products(i + 1, j)
                if j % 2 == 0:
                    exponentials(i, j // 2)

    waits1, waits2 = {}, {}

    def stats_local(c):
        d = rows(c)
        for k in range(2):
            peaks = [stat[t, k : k + 1, d] for t in range(tiles)]
            sums = [stat[t, 2 + k : 3 + k, d] for t in range(tiles)]
            peak = functools.reduce(jnp.maximum, peaks)
            total = functools.reduce(jnp.add, [s * jnp.exp2(m - peak) for s, m in zip(sums, peaks)])
            value = peak + jnp.log(total) * LOG2E
            for n in range(4):
                sb1[c, 4 * k + n : 4 * k + n + 1, :] = value[:, n * 128 : (n + 1) * 128]
        waits1[c] = spread(sb1.at[c], s1.at[c], peers1, lambda n: s1.at[c, n])

    def stats_middle(c):
        waits1[c].wait_recv()
        sb2[c] = log_total([sb1[c]] + [s1[c, n] for n in range(STATS - 1)])
        waits2[c] = spread(sb2.at[c], s2.at[c], peers2, lambda n: s2.at[c, n])

    def stats_final(c):
        waits2[c].wait_recv()
        lse[c] = log_total([sb2[c]] + [s2[c, n] for n in range(STATS - 1)])
        d = rows(c)
        lse_s, lse_t = wide(lse[c, 0:4, :]), wide(lse[c, 4:8, :])
        part = (1.5 * lse_s - lse_t) * (1.0 / 64.0)
        for t in range(tiles):
            part = part + stat[t, 4:5, d] * jnp.exp2(stat[t, 1:2, d] - lse_t) - CE_WEIGHT * stat[t, 5:6, d]
            stat[t, 6:7, d] = (1.0 + CE_WEIGHT) * jnp.exp2(stat[t, 0:1, d] - lse_s)
            stat[t, 7:8, d] = jnp.exp2(stat[t, 1:2, d] - lse_t)
        lacc[c : c + 1, :] = part

    def logit_grads(c):
        d = rows(c)
        positive = pos_ref[0:1, d] - p * passages

        @pl.loop(0, tiles)
        def _(t):
            r = pl.ds(pl.multiple_of(t * TILE, TILE), TILE)
            row = lax.broadcasted_iota(jnp.int32, (TILE, CHUNK), 0) + t * TILE
            v = es[r, d] * stat[t, 6:7, d] - et[r, d] * stat[t, 7:8, d]
            g[r, d] = jnp.where(row == positive, v - CE_WEIGHT, v).astype(jnp.bfloat16)

    def query_terms(c):
        own[rows(c), :] = dot(g[:, rows(c)], sp[...], TN)

    pas_rows = passages // 2
    pas_sent = []

    def passage_send(b):
        n = TILE
        ps[pl.ds(b * n, n), :] = dot(g[pl.ds(pl.multiple_of((1 - q) * pas_rows + b * n, n), n), :], sq[...], NN)
        pas_sent.append(post(ps.at[pl.ds(b * n, n)], pr.at[pl.ds(b * n, n)], other))

    def passage_own(b):
        n = TILE
        pas[pl.ds(b * n, n), :] = dot(g[pl.ds(pl.multiple_of(q * pas_rows + b * n, n), n), :], sq[...], NN)

    def passage_add(b):
        n = TILE
        pas_sent[b].wait_recv()
        r = pl.ds(b * n, n)
        pas[r, :] = (pas[r, :] + pr[r, :]) * (scale * passages * lax.axis_size("pass"))

    size = queries // CHUNKS
    piece, block, slab = size // 16, size // 64, size // 4
    hp = piece // 2

    def query_sum(c):
        base = c * size // 2

        def cut(s, j, h=None):
            at = base + s * slab + j * piece + (0 if h is None else h * hp)
            return half.at[pl.ds(aligned(at, hp), piece if h is None else hp)]

        def add(ref, *others):
            ref[...] = functools.reduce(jnp.add, [o[...] for o in others], ref[...])

        def far(s, k):
            return rfar.at[pl.ds(((c * 2 + s) * 6 + k) * hp, hp)]

        index = ((y, z), (z, y))

        def step(s, axis, d):
            along_y = (s == 0) == (axis == 0)
            return dev(yy=(y + d) % 4) if along_y else dev(zz=(z + d) % 4)

        first = post(
            own.at[pl.ds(aligned(c * size + (1 - core) * (size // 2), size // 2), size // 2)],
            half.at[pl.ds(base, size // 2)],
            partner,
        )
        yield
        first.wait_recv()
        mine = pl.ds(aligned(c * size + core * (size // 2), size // 2), size // 2)
        half[pl.ds(base, size // 2), :] = half[pl.ds(base, size // 2), :] + own[mine, :]
        w = {}
        for s in range(2):
            i = index[s][0]
            right, left = step(s, 0, 1), step(s, 0, 3)
            w[s, 0] = post(cut(s, (i + 2) % 4, 0), far(s, 0), right)
            w[s, 1] = post(cut(s, (i + 2) % 4, 1), far(s, 1), left)
            w[s, 2] = post(cut(s, (i + 1) % 4, 1), far(s, 2), right)
            w[s, 3] = post(cut(s, (i + 3) % 4, 0), far(s, 3), left)
        yield
        for s in range(2):
            i = index[s][0]
            right, left = step(s, 0, 1), step(s, 0, 3)
            w[s, 0].wait_recv()
            add(cut(s, (i + 1) % 4, 0), far(s, 0))
            w[s, 4] = post(cut(s, (i + 1) % 4, 0), far(s, 4), right)
            w[s, 1].wait_recv()
            add(cut(s, (i + 3) % 4, 1), far(s, 1))
            w[s, 5] = post(cut(s, (i + 3) % 4, 1), far(s, 5), left)
        yield

        def near(s, d):
            return rnear.at[pl.ds(((c * 2 + s) * 3 + d - 1) * block, block)]

        def small(s, j):
            at = base + s * slab + index[s][0] * piece + j * block
            return half.at[pl.ds(aligned(at, block), block)]

        for s in range(2):
            i, j = index[s]
            for k in range(2, 6):
                w[s, k].wait_recv()
            add(cut(s, i, 0), far(s, 3), far(s, 4))
            add(cut(s, i, 1), far(s, 2), far(s, 5))
            for d in range(1, 4):
                w[s, 5 + d] = post(small(s, (j + d) % 4), near(s, d), step(s, 1, d))
        yield

        def over(s):
            return rx.at[pl.ds((c * 2 + s) * block, block)]

        for s in range(2):
            j = index[s][1]
            for d in range(1, 4):
                w[s, 5 + d].wait_recv()
            add(small(s, j), *[near(s, d) for d in range(1, 4)])
            w[s, 9] = post(small(s, j), over(s), across)
        yield

        def place(s, i, j=0, n=piece):
            at = c * size + core * (size // 2) + s * slab + i * piece + j * block
            return out.at[pl.ds(aligned(at, min(n, block)), n)]

        for s in range(2):
            i, j = index[s]
            w[s, 9].wait_recv()
            here = place(s, i, j, block)
            here[...] = (small(s, j)[...] + over(s)[...]) * scale
            for d in range(1, 4):
                w[s, 9 + d] = post(here, here, step(s, 1, d))
        yield
        for s in range(2):
            i = index[s][0]
            for d in range(1, 4):
                w[s, 9 + d].wait_recv()
            w[s, 13] = post(place(s, i), place(s, i), step(s, 0, 1))
            w[s, 14] = post(place(s, i), place(s, i), step(s, 0, 3))
        yield

        def part(s, i, h):
            at = c * size + core * (size // 2) + s * slab + i * piece + h * hp
            return out.at[pl.ds(aligned(at, hp), hp)]

        for s in range(2):
            i = index[s][0]
            w[s, 13].wait_recv()
            w[s, 15] = post(part(s, (i + 3) % 4, 0), part(s, (i + 3) % 4, 0), step(s, 0, 1))
            w[s, 14].wait_recv()
            w[s, 16] = post(part(s, (i + 1) % 4, 1), part(s, (i + 1) % 4, 1), step(s, 0, 3))
        yield
        for s in range(2):
            w[s, 15].wait_recv()
            w[s, 16].wait_recv()
            done = out.at[pl.ds(aligned(c * size + core * (size // 2) + s * slab, slab), slab)]
            w[s, 17] = post(done, done, partner)
        yield
        for s in range(2):
            w[s, 17].wait_recv()
        yield

    def loss_sum():
        i1, i2 = core * 4 + y, xh * 4 + z
        total = jnp.sum(lacc[0:CHUNKS, :], axis=0, keepdims=True)
        total = functools.reduce(jnp.add, [total[:, n * 128 : (n + 1) * 128] for n in range(CHUNK // 128)])
        lb1[i1] = jnp.broadcast_to(total, (8, 128))
        wait = spread(lb1.at[i1], lb1, peers1, lambda n: lb1.at[i1])
        yield
        wait.wait_recv()
        lb2[i2] = functools.reduce(jnp.add, [lb1[n] for n in range(STATS)])
        wait = spread(lb2.at[i2], lb2, peers2, lambda n: lb2.at[i2])
        yield
        wait.wait_recv()
        lb3[0] = functools.reduce(jnp.add, [lb2[n] for n in range(STATS)])
        last = post(lb3.at[0], lb3.at[1], other)
        yield
        last.wait_recv()
        value = jnp.sum(lb3[0, 0:1, :] + lb3[1, 0:1, :], axis=1, keepdims=True) * (LN2 / (2 * queries))
        loss_ref[...] = jnp.broadcast_to(value, loss_ref.shape)
        yield

    for j in range(4):
        products(0, j)
    for c in range(CHUNKS):
        logits(c)
        if c == 0:
            pl.semaphore_wait(barrier, len(everyone))
        stats_local(c)
        if c >= 1:
            stats_middle(c - 1)
    sums = [query_sum(c) for c in range(CHUNKS)]
    loss = loss_sum()

    def compute(c):
        stats_final(c)
        logit_grads(c)
        query_terms(c)
        next(sums[c])

    compute(0)
    stats_middle(CHUNKS - 1)
    compute(1)
    next(sums[0])
    compute(2)
    next(sums[1])
    compute(3)
    next(sums[2])
    next(sums[0])
    for b in range(2):
        passage_send(b)
        next(sums[3 - 2 * b])
    next(loss)
    for b in range(2):
        passage_own(b)
        next(sums[b])
    stages = {0: 4, 1: 4, 2: 2, 3: 2}
    for tick in range(4, 20):
        for c in range(CHUNKS):
            while stages[c] < 10 and stages[c] + 2 * c <= tick:
                next(sums[c])
                stages[c] += 1
        if 6 <= tick < 9:
            next(loss)
    passage_add(0)
    passage_add(1)
    for copy in sent:
        copy.wait_send()


def shards(student_queries, teacher_queries, student_passages, teacher_passages, positives):
    queries, ds = student_queries.shape
    passages, dt = teacher_passages.shape
    f32, bf16 = jnp.float32, jnp.bfloat16
    vmem = pltpu.VMEM
    size = queries // CHUNKS
    scratch = [
        vmem((queries, ds), bf16),
        vmem((queries, dt), bf16),
        vmem((passages, ds), bf16),
        vmem((passages, dt), bf16),
        vmem((passages, queries), f32),
        vmem((passages, queries), f32),
        vmem((passages // TILE, 8, queries), f32),
        *[vmem((TILE, CHUNK), f32), vmem((TILE, CHUNK), f32), vmem((2, 8, CHUNK), f32)] * 2,
        vmem((passages, queries), bf16),
        vmem((queries, ds), f32),
        vmem((queries // 2, ds), f32),
        vmem((CHUNKS * 2 * 6 * (size // 32), ds), f32),
        vmem((CHUNKS * 2 * 3 * (size // 64), ds), f32),
        vmem((CHUNKS * 2 * (size // 64), ds), f32),
        vmem((passages // 2, ds), f32),
        vmem((passages // 2, ds), f32),
        vmem((CHUNKS, 8, 128), f32),
        vmem((CHUNKS, STATS - 1, 8, 128), f32),
        vmem((CHUNKS, 8, 128), f32),
        vmem((CHUNKS, STATS - 1, 8, 128), f32),
        vmem((CHUNKS, 8, 128), f32),
        vmem((STATS, 8, 128), f32),
        vmem((STATS, 8, 128), f32),
        vmem((2, 8, 128), f32),
        vmem((8, CHUNK), f32),
        pltpu.SemaphoreType.DMA((180,)),
        pltpu.SemaphoreType.DMA((180,)),
        pltpu.SemaphoreType.DMA((2 + 2 * CHUNKS,)),
    ]
    loss, query_grads, passage_grads = pl.pallas_call(
        kernel,
        out_shape=(
            jax.ShapeDtypeStruct((8, 128), f32),
            jax.ShapeDtypeStruct((queries, ds), f32),
            jax.ShapeDtypeStruct((passages // 2, ds), f32),
        ),
        in_specs=[pl.BlockSpec(memory_space=pl.ANY)] * 4 + [pl.BlockSpec(memory_space=vmem)],
        out_specs=[pl.BlockSpec(memory_space=vmem)] * 3,
        scratch_shapes=scratch,
        compiler_params=pltpu.CompilerParams(collective_id=0, has_side_effects=True, vmem_limit_bytes=62 * 2**20),
        cost_estimate=pl.CostEstimate(flops=14 * 10**9, bytes_accessed=20 * 10**6, transcendentals=4 * 10**6),
    )(student_queries, teacher_queries, student_passages, teacher_passages, positives.reshape(1, queries))
    return loss[0, 0], query_grads, passage_grads


def solution(mesh):
    return jax.shard_map(
        shards,
        mesh=mesh,
        in_specs=(P("qry", None), P("qry", None), P("pass", None), P("pass", None), P("qry")),
        out_specs=(P(), P("qry", None), P(("pass", "qry"), None)),
        check_vma=False,
    )
```

time: 1410 us -> 132 us (0.09)
  waiting for transfers between devices: 672 us -> 0 us
  blocking collectives: 659 us -> 0 us
  Pallas kernels: 0 us -> 123 us
  matrix products: 35.3 us -> 0 us
  between operations: 17.3 us -> 0.64 us
  other arithmetic: 16 us -> 0 us
    psum x1 -> x0, waiting for transfers between devices: 638 us -> none  [shards(): query_grads = lax.psum(local_grads, 'pass')]
    pmax x2 -> x0, blocking collectives: 338 us -> none  [shards(): lax.pmax((jnp.max(student_logits, axis=1), jnp.max(teacher_logits, axis=1...]
    psum x2 -> x0, blocking collectives: 321 us -> none  [the longest x1 316 us: shards(): lax.psum((jnp.sum(jnp.exp(student_logits - student_peak[:, None]), axis=1...]
    pallas_call x0 -> x1, Pallas kernels: none -> 123 us  [shards(): pl.pallas_call(kernel, out_shape=(jax.ShapeDtypeStruct((8, 128), f32), ja...]
    dot_general x4 -> x0, matrix products: 35.3 us -> none  [the longest x1 10.8 us: shards(): lax.dot_general(teacher_queries, teacher_passages, contract_last, preferr...]
    reduce_scatter x1 -> x0, waiting for transfers between devices: 33.5 us -> none  [shards(): lax.psum_scatter(passage_terms, 'qry', scatter_dimension=0, tiled=True)]
  transfers between devices with their start and end apart: 2 -> 0, of which waited for: 2 -> 0; matrix products, arithmetic and copies ran while one was open for 1% -> 0% of each run, Pallas kernels for 0% -> 0%
where the time goes in v1:
time: 132 us
  Pallas kernels  123 us (93%)
  local copies, waits for them, and re-layouts  8.34 us (6%)
    pallas_call x1, Pallas kernels, shards(): pl.pallas_call(kernel, out_shape=(jax.ShapeDtypeStruct((8, 128), f32), ja...  123 us
    unnamed x4, local copies, waits for them, and re-layouts  7.16 us

profile of v1, /device:TPU:1, one launch (start us, length us, event | category | flops | bytes accessed | tf_op | source)
XLA Modules:
  0.0 132.1 jit_solution(14289813917283847639)
XLA Ops:
  0.6 123.2 %shard_map.76 = (f32[8,128]{1,0:T(8,128)}, f32[2048,768]{1,0:T(8,128)}, f32[512,768]{1,0:T(8,128)}) custom-call(bf16[2048,768]{1,0:T(8,128)(2,1)} %sq_hbm.1, bf16[2048,1024]{1,0:T(8,128)(2,1)} %tq_hbm.1, bf16[1024,768]{1,0:T(8,128)(2,1)} %sp_hbm.1, bf16[1024,1024]{1,0:T(8,128)(2,1)} %tp_hbm.1, s32[1,2048]{1,0:T(1,128)} %bitcast.2), custom_call_target="tpu_custom_call" | custom-call | flops 14000000000 | bytes 20000000 | tf_op jit(solution)/shard_map/pallas_call | solution.py:455
  123.8 1.2 slice.3
  125.0 0.0 copy-start
  125.0 6.0 %copy.10 = f32[2048,768]{1,0:T(8,128)} copy(f32[2048,768]{1,0:T(8,128)} %get-tuple-element.13) | data formatting | bytes 12582912
  131.0 0.0 copy-done
  131.0 1.1 copy.11
Async XLA Ops:
  125.0 6.0 %copy-start = (f32[512,768]{1,0:T(8,128)S(1)}, f32[512,768]{1,0:T(8,128)}, u32[]{:S(2)}) copy-start(f32[512,768]{1,0:T(8,128)} %get-tuple-element.14) | copy-start | bytes 4718596

commit v2 on v1

--- a/solution.py
+++ b/solution.py
@@ -20,6 +20,8 @@
 CHUNK = 512
 CHUNKS = 4
 STATS = 8
+ROUNDS = 2
+PARTS = (128, 64, 128, 64, 128)
 
 
 def dot(a, b, dims):
@@ -165,35 +167,41 @@
                     exponentials(i, j // 2)
 
     waits1, waits2 = {}, {}
-
-    def stats_local(c):
-        d = rows(c)
-        for k in range(2):
-            peaks = [stat[t, k : k + 1, d] for t in range(tiles)]
-            sums = [stat[t, 2 + k : 3 + k, d] for t in range(tiles)]
-            peak = functools.reduce(jnp.maximum, peaks)
-            total = functools.reduce(jnp.add, [s * jnp.exp2(m - peak) for s, m in zip(sums, peaks)])
-            value = peak + jnp.log(total) * LOG2E
-            for n in range(4):
-                sb1[c, 4 * k + n : 4 * k + n + 1, :] = value[:, n * 128 : (n + 1) * 128]
-        waits1[c] = spread(sb1.at[c], s1.at[c], peers1, lambda n: s1.at[c, n])
-
-    def stats_middle(c):
-        waits1[c].wait_recv()
-        sb2[c] = log_total([sb1[c]] + [s1[c, n] for n in range(STATS - 1)])
-        waits2[c] = spread(sb2.at[c], s2.at[c], peers2, lambda n: s2.at[c, n])
-
-    def stats_final(c):
-        waits2[c].wait_recv()
-        lse[c] = log_total([sb2[c]] + [s2[c, n] for n in range(STATS - 1)])
-        d = rows(c)
-        lse_s, lse_t = wide(lse[c, 0:4, :]), wide(lse[c, 4:8, :])
-        part = (1.5 * lse_s - lse_t) * (1.0 / 64.0)
-        for t in range(tiles):
-            part = part + stat[t, 4:5, d] * jnp.exp2(stat[t, 1:2, d] - lse_t) - CE_WEIGHT * stat[t, 5:6, d]
-            stat[t, 6:7, d] = (1.0 + CE_WEIGHT) * jnp.exp2(stat[t, 0:1, d] - lse_s)
-            stat[t, 7:8, d] = jnp.exp2(stat[t, 1:2, d] - lse_t)
-        lacc[c : c + 1, :] = part
+    per = CHUNKS // ROUNDS
+
+    def stats_local(r):
+        for n in range(per):
+            d = rows(r * per + n)
+            for k in range(2):
+                peaks = [stat[t, k : k + 1, d] for t in range(tiles)]
+                sums = [stat[t, 2 + k : 3 + k, d] for t in range(tiles)]
+                peak = functools.reduce(jnp.maximum, peaks)
+                total = functools.reduce(jnp.add, [s * jnp.exp2(m - peak) for s, m in zip(sums, peaks)])
+                value = peak + jnp.log(total) * LOG2E
+                for m in range(4):
+                    at = (k * per + n) * 4 + m
+                    sb1[r, at : at + 1, :] = value[:, m * 128 : (m + 1) * 128]
+        waits1[r] = spread(sb1.at[r], s1.at[r], peers1, lambda n: s1.at[r, n])
+
+    def stats_middle(r):
+        waits1[r].wait_recv()
+        sb2[r] = log_total([sb1[r]] + [s1[r, n] for n in range(STATS - 1)])
+        waits2[r] = spread(sb2.at[r], s2.at[r], peers2, lambda n: s2.at[r, n])
+
+    def stats_final(r):
+        waits2[r].wait_recv()
+        lse[r] = log_total([sb2[r]] + [s2[r, n] for n in range(STATS - 1)])
+        for n in range(per):
+            c = r * per + n
+            d = rows(c)
+            lse_s = wide(lse[r, n * 4 : n * 4 + 4, :])
+            lse_t = wide(lse[r, (per + n) * 4 : (per + n) * 4 + 4, :])
+            part = (1.5 * lse_s - lse_t) * (1.0 / 64.0)
+            for t in range(tiles):
+                part = part + stat[t, 4:5, d] * jnp.exp2(stat[t, 1:2, d] - lse_t) - CE_WEIGHT * stat[t, 5:6, d]
+                stat[t, 6:7, d] = (1.0 + CE_WEIGHT) * jnp.exp2(stat[t, 0:1, d] - lse_s)
+                stat[t, 7:8, d] = jnp.exp2(stat[t, 1:2, d] - lse_t)
+            lacc[c : c + 1, :] = part
 
     def logit_grads(c):
         d = rows(c)
@@ -212,19 +220,26 @@
     pas_rows = passages // 2
     pas_sent = []
 
-    def passage_send(b):
-        n = TILE
-        ps[pl.ds(b * n, n), :] = dot(g[pl.ds(pl.multiple_of((1 - q) * pas_rows + b * n, n), n), :], sq[...], NN)
-        pas_sent.append(post(ps.at[pl.ds(b * n, n)], pr.at[pl.ds(b * n, n)], other))
-
-    def passage_own(b):
-        n = TILE
-        pas[pl.ds(b * n, n), :] = dot(g[pl.ds(pl.multiple_of(q * pas_rows + b * n, n), n), :], sq[...], NN)
-
-    def passage_add(b):
-        n = TILE
-        pas_sent[b].wait_recv()
-        r = pl.ds(b * n, n)
+    def passage_terms(into, first, b, r):
+        n, k = TILE, queries // ROUNDS
+        at = pl.ds(pl.multiple_of(first + b * n, n), n)
+        term = dot(g[at, pl.ds(r * k, k)], sq[pl.ds(r * k, k), :], NN)
+        to = pl.ds(b * n, n)
+        into[to, :] = term if r == 0 else into[to, :] + term
+
+    def passage_send(b, r):
+        passage_terms(ps, (1 - q) * pas_rows, b, r)
+
+    def passage_own(b, r):
+        passage_terms(pas, q * pas_rows, b, r)
+
+    def passage_post(n):
+        r = pl.ds(sum(PARTS[:n]), PARTS[n])
+        pas_sent.append(post(ps.at[r], pr.at[r], other))
+
+    def passage_add(n):
+        pas_sent[n].wait_recv()
+        r = pl.ds(sum(PARTS[:n]), PARTS[n])
         pas[r, :] = (pas[r, :] + pr[r, :]) * (scale * passages * lax.axis_size("pass"))
 
     size = queries // CHUNKS
@@ -305,6 +320,7 @@
                 w[s, 5 + d].wait_recv()
             add(small(s, j), *[near(s, d) for d in range(1, 4)])
             w[s, 9] = post(small(s, j), over(s), across)
+        passage_post(len(pas_sent))
         yield
 
         def place(s, i, j=0, n=piece):
@@ -368,50 +384,60 @@
         loss_ref[...] = jnp.broadcast_to(value, loss_ref.shape)
         yield
 
+    sums = [query_sum(c) for c in range(CHUNKS)]
+    loss = loss_sum()
     for j in range(4):
         products(0, j)
-    for c in range(CHUNKS):
-        logits(c)
-        if c == 0:
-            pl.semaphore_wait(barrier, len(everyone))
-        stats_local(c)
-        if c >= 1:
-            stats_middle(c - 1)
-    sums = [query_sum(c) for c in range(CHUNKS)]
-    loss = loss_sum()
-
-    def compute(c):
-        stats_final(c)
-        logit_grads(c)
-        query_terms(c)
-        next(sums[c])
-
-    compute(0)
-    stats_middle(CHUNKS - 1)
-    compute(1)
+    logits(0)
+    logits(1)
+    pl.semaphore_wait(barrier, len(everyone))
+    stats_local(0)
+    logits(2)
+    stats_middle(0)
+    logits(3)
+    stats_local(1)
+    stats_final(0)
+    logit_grads(0)
+    query_terms(0)
     next(sums[0])
-    compute(2)
+    logit_grads(1)
+    query_terms(1)
     next(sums[1])
-    compute(3)
+    stats_middle(1)
+    next(sums[0])
+    passage_send(0, 0)
+    passage_send(1, 0)
+    next(sums[1])
+    passage_own(0, 0)
+    passage_own(1, 0)
+    next(sums[0])
+    stats_final(1)
+    logit_grads(2)
+    logit_grads(3)
+    passage_send(0, 1)
+    passage_post(0)
+    passage_send(1, 1)
+    next(sums[1])
+    query_terms(2)
     next(sums[2])
+    query_terms(3)
+    next(sums[3])
     next(sums[0])
-    for b in range(2):
-        passage_send(b)
-        next(sums[3 - 2 * b])
-    next(loss)
-    for b in range(2):
-        passage_own(b)
-        next(sums[b])
+    passage_own(0, 1)
+    next(sums[2])
+    passage_own(1, 1)
+    next(sums[1])
+    next(sums[3])
     stages = {0: 4, 1: 4, 2: 2, 3: 2}
     for tick in range(4, 20):
         for c in range(CHUNKS):
-            while stages[c] < 10 and stages[c] + 2 * c <= tick:
+            while stages[c] < 10 and stages[c] + c <= tick:
                 next(sums[c])
                 stages[c] += 1
-        if 6 <= tick < 9:
+        if 7 <= tick < 11:
             next(loss)
-    passage_add(0)
-    passage_add(1)
+    for n in range(len(PARTS)):
+        passage_add(n)
     for copy in sent:
         copy.wait_send()
 
@@ -439,11 +465,11 @@
         vmem((CHUNKS * 2 * (size // 64), ds), f32),
         vmem((passages // 2, ds), f32),
         vmem((passages // 2, ds), f32),
-        vmem((CHUNKS, 8, 128), f32),
-        vmem((CHUNKS, STATS - 1, 8, 128), f32),
-        vmem((CHUNKS, 8, 128), f32),
-        vmem((CHUNKS, STATS - 1, 8, 128), f32),
-        vmem((CHUNKS, 8, 128), f32),
+        vmem((ROUNDS, 16, 128), f32),
+        vmem((ROUNDS, STATS - 1, 16, 128), f32),
+        vmem((ROUNDS, 16, 128), f32),
+        vmem((ROUNDS, STATS - 1, 16, 128), f32),
+        vmem((ROUNDS, 16, 128), f32),
         vmem((STATS, 8, 128), f32),
         vmem((STATS, 8, 128), f32),
         vmem((2, 8, 128), f32),
@@ -456,13 +482,13 @@
         kernel,
         out_shape=(
             jax.ShapeDtypeStruct((8, 128), f32),
-            jax.ShapeDtypeStruct((queries, ds), f32),
-            jax.ShapeDtypeStruct((passages // 2, ds), f32),
+            vmem((queries, ds), f32),
+            vmem((passages // 2, ds), f32),
         ),
         in_specs=[pl.BlockSpec(memory_space=pl.ANY)] * 4 + [pl.BlockSpec(memory_space=vmem)],
         out_specs=[pl.BlockSpec(memory_space=vmem)] * 3,
         scratch_shapes=scratch,
-        compiler_params=pltpu.CompilerParams(collective_id=0, has_side_effects=True, vmem_limit_bytes=62 * 2**20),
+        compiler_params=pltpu.CompilerParams(collective_id=0, has_side_effects=True, vmem_limit_bytes=52 * 2**20),
         cost_estimate=pl.CostEstimate(flops=14 * 10**9, bytes_accessed=20 * 10**6, transcendentals=4 * 10**6),
     )(student_queries, teacher_queries, student_passages, teacher_passages, positives.reshape(1, queries))
     return loss[0, 0], query_grads, passage_grads

time: 132 us -> 91.7 us (0.69)
  Pallas kernels: 123 us -> 85.9 us
  local copies, waits for them, and re-layouts: 8.34 us -> 5.03 us
    pallas_call x1, Pallas kernels: 123 us -> 85.9 us  [shards(): pl.pallas_call(kernel, out_shape=(jax.ShapeDtypeStruct((8, 128), f32), vm...]
    unnamed x4 -> x2, local copies, waits for them, and re-layouts: 7.16 us -> 3.84 us
where the time goes in v2:
time: 91.7 us; the launch traced here: 91.5 us
  Pallas kernels  85.9 us (94%)
  local copies, waits for them, and re-layouts  5.03 us (5%)
    pallas_call x1, Pallas kernels, shards(): pl.pallas_call(kernel, out_shape=(jax.ShapeDtypeStruct((8, 128), f32), vm...  85.9 us
    unnamed x2, local copies, waits for them, and re-layouts  3.84 us

profile of v2, /device:TPU:1, one launch (start us, length us, event | category | flops | bytes accessed | tf_op | source)
XLA Modules:
  0.0 91.5 jit_solution(9067491005762624043)
XLA Ops:
  0.6 85.9 %shard_map.76 = (f32[8,128]{1,0:T(8,128)}, f32[2048,768]{1,0:T(8,128)S(1)}, f32[512,768]{1,0:T(8,128)S(1)}) custom-call(bf16[2048,768]{1,0:T(8,128)(2,1)} %sq_hbm.1, bf16[2048,1024]{1,0:T(8,128)(2,1)} %tq_hbm.1, bf16[1024,768]{1,0:T(8,128)(2,1)} %sp_hbm.1, bf16[1024,1024]{1,0:T(8,128)(2,1)} %tp_hbm.1, s32[1,2048]{1,0:T(1,128)} %bitcast.2), custom_call_target="tpu_custom_call" | custom-call | flops 14000000000 | bytes 20000000 | tf_op jit(solution)/shard_map/pallas_call | solution.py:481
  86.5 1.2 %slice.3 = f32[1,1]{1,0:T(1,128)} slice(f32[8,128]{1,0:T(8,128)} %get-tuple-element.6), slice={[0:1], [0:1]} | slice | bytes 8 | tf_op jit(solution)/shard_map/slice | solution.py:494
  87.7 1.1 %copy.11 = f32[512,768]{1,0:T(8,128)} copy(f32[512,768]{1,0:T(8,128)S(1)} %get-tuple-element.11) | data formatting | bytes 3145728
  88.8 2.7 %copy.10 = f32[2048,768]{1,0:T(8,128)} copy(f32[2048,768]{1,0:T(8,128)S(1)} %get-tuple-element.10) | data formatting | bytes 12582912

commit v3 on v2

--- a/solution.py
+++ b/solution.py
@@ -18,10 +18,15 @@
 NN = (((1,), (0,)), ((), ()))
 TILE = 256
 CHUNK = 512
+UNIT = 256
 CHUNKS = 4
 STATS = 8
 ROUNDS = 2
-PARTS = (128, 64, 128, 64, 128)
+EVENTS = (
+    6, 0, 1, 7, 0, 2, 1, 3, 4, -64, 0, 2, 8, 1, -32, 3, 8, 9, 2, -32, 9, 9, 1, 3, -32, 9, 9, 0, 2, 9, 9, 9, 3, 0, -32,
+    5, 1, -32, 0, -32, 5, 2, -32, 3, 1, 0, -32, 5, 2, -32, 0, 3, 1, -32, 2, -32, 5, 3, -32, 1, 2, -32, 1, 3, 2, -32, 3,
+)
+PARTS = tuple(-e for e in EVENTS if e < 0)
 
 
 def dot(a, b, dims):
@@ -44,8 +49,8 @@
 
 def kernel(
     sq_hbm, tq_hbm, sp_hbm, tp_hbm, pos_ref, loss_ref, out, pas,
-    sq, tq, sp, tp, es, et, stat, bs0, bt0, mx0, bs1, bt1, mx1, g, own, half, rfar, rnear, rx, ps, pr,
-    sb1, s1, sb2, s2, lse, lb1, lb2, lb3, lacc, ssem, rsem, lsem,
+    sq, tq, sp, tp, raw_s, raw_t, peaks, totals, g, own, half, rfar, rnear, rx, ps, pr,
+    sb1, s1, sb2, s2, lse, lses, lb1, lb2, lb3, lacc, ssem, rsem, lsem,
 ):
     queries, ds = sq.shape
     passages, dt = tp.shape
@@ -53,6 +58,7 @@
     ct = LOGIT_GAIN / math.sqrt(dt) * LOG2E
     scale = LOGIT_GAIN / math.sqrt(ds)
     tiles = passages // TILE
+    units = 2 * (queries // UNIT)
     p, q = lax.axis_index("pass"), lax.axis_index("qry")
     core, y, z, xh = p % 2, (p // 2) % 4, (p // 8) % 4, p // 32
 
@@ -68,13 +74,21 @@
     def rows(c):
         return pl.ds(c * CHUNK, CHUNK)
 
-    load("sp", sp_hbm, sp)
-    load("sq0", sq_hbm.at[rows(0)], sq.at[rows(0)])
-    load("tp", tp_hbm, tp)
-    load("tq0", tq_hbm.at[rows(0)], tq.at[rows(0)])
+    def unit(b):
+        return pl.ds(b * UNIT, UNIT)
+
+    top, bottom = pl.ds(0, passages // 2), pl.ds(passages // 2, passages // 2)
+    load("s0", sp_hbm.at[top], sp.at[top])
+    load("sq0", sq_hbm.at[unit(0)], sq.at[unit(0)])
+    load("s1", sp_hbm.at[bottom], sp.at[bottom])
+    load("t0", tp_hbm.at[top], tp.at[top])
+    load("tq0", tq_hbm.at[unit(0)], tq.at[unit(0)])
+    load("t1", tp_hbm.at[bottom], tp.at[bottom])
+    load("sq1", sq_hbm.at[unit(1)], sq.at[unit(1)])
+    load("tq1", tq_hbm.at[unit(1)], tq.at[unit(1)])
     for c in range(1, CHUNKS):
-        load(f"sq{c}", sq_hbm.at[rows(c)], sq.at[rows(c)])
-        load(f"tq{c}", tq_hbm.at[rows(c)], tq.at[rows(c)])
+        load(f"sq{2 * c}", sq_hbm.at[rows(c)], sq.at[rows(c)])
+        load(f"tq{2 * c}", tq_hbm.at[rows(c)], tq.at[rows(c)])
 
     group1 = [(a, b) for a in range(2) for b in range(4) if (a, b) != (0, 0)]
     peers1 = [dev(c=(core + a) % 2, yy=(y + b) % 4) for a, b in group1]
@@ -118,69 +132,47 @@
         sent.append(both)
         return both
 
-    buffers = ((bs0, bt0, mx0), (bs1, bt1, mx1))
-
-    def products(i, piece):
-        c, t = divmod(i, tiles)
-        bs, bt, mx = buffers[i % 2]
-        teacher, j = divmod(piece, 2)
-        w = CHUNK // 2
-        if t == 0 and j == 0:
-            if c == 0:
-                loads["tp" if teacher else "sp"].wait()
-            loads[f"{'tq' if teacher else 'sq'}{c}"].wait()
-        a = (tp if teacher else sp)[pl.ds(t * TILE, TILE), :]
-        b = (tq if teacher else sq)[pl.ds(c * CHUNK + j * w, w), :]
-        r = dot(a, b, NT)
-        (bt if teacher else bs)[:, j * w : (j + 1) * w] = r
-        mx[teacher, :, j * w : (j + 1) * w] = jnp.max(r.reshape(TILE // 8, 8, w), axis=0)
-
-    def exponentials(i, j):
-        c, t = divmod(i, tiles)
-        bs, bt, mx = buffers[i % 2]
-        w = CHUNK // 2
-        cut = slice(j * w, (j + 1) * w)
-        d = pl.ds(c * CHUNK + j * w, w)
-        s2 = bs[:, cut] * cs
-        t2 = bt[:, cut] * ct
-        ms = jnp.max(mx[0, :, cut], axis=0, keepdims=True) * cs
-        mt = jnp.max(mx[1, :, cut], axis=0, keepdims=True) * ct
-        e_s = jnp.exp2(s2 - ms)
-        e_t = jnp.exp2(t2 - mt)
-        row = lax.broadcasted_iota(jnp.int32, (TILE, w), 0) + t * TILE
-        at_positive = jnp.where(row == pos_ref[0:1, d] - p * passages, s2, 0.0)
-        es[pl.ds(t * TILE, TILE), d] = e_s
-        et[pl.ds(t * TILE, TILE), d] = e_t
-        stat[t, 0:1, d] = ms
-        stat[t, 1:2, d] = mt
-        stat[t, 2:3, d] = jnp.sum(e_s, axis=0, keepdims=True)
-        stat[t, 3:4, d] = jnp.sum(e_t, axis=0, keepdims=True)
-        stat[t, 4:5, d] = jnp.sum(e_t * (t2 - s2), axis=0, keepdims=True)
-        stat[t, 5:6, d] = jnp.sum(at_positive, axis=0, keepdims=True)
-
-    def logits(c):
-        for i in range(c * tiles, (c + 1) * tiles):
-            for j in range(4):
-                if i + 1 < CHUNKS * tiles:
-                    products(i + 1, j)
-                if j % 2 == 0:
-                    exponentials(i, j // 2)
+    raws, sides, factors = (raw_s, raw_t), ((sp, sq), (tp, tq)), (cs, ct)
+
+    def products(u, j):
+        b, k = divmod(u, 2)
+        if b == 0:
+            loads[f"{'st'[k]}{j}"].wait()
+        if j == 0 and f"{'st'[k]}q{b}" in loads:
+            loads[f"{'st'[k]}q{b}"].wait()
+        half_rows = pl.ds(j * (passages // 2), passages // 2)
+        d = unit(b)
+        r = dot(sides[k][0][half_rows, :], sides[k][1][d, :], NT)
+        raws[k][half_rows, d] = r
+        m = jnp.max(r.reshape(passages // 16, 8, UNIT), axis=0)
+        peaks[k, :, d] = m if j == 0 else jnp.maximum(peaks[k, :, d], m)
+
+    def exponentials(u, j):
+        b, k = divmod(u, 2)
+        d = unit(b)
+        m = jnp.max(peaks[k, :, d], axis=0, keepdims=True) * factors[k]
+        e = jnp.exp2(raws[k][pl.ds(j * TILE, TILE), d] * factors[k] - m)
+        total = jnp.sum(e.reshape(TILE // 8, 8, UNIT), axis=0)
+        totals[k, :, d] = total if j == 0 else totals[k, :, d] + total
+
+    def logits(u):
+        for j in range(tiles):
+            if u < units and j % 2 == 0:
+                products(u, j // 2)
+            if u > 0:
+                exponentials(u - 1, j)
 
     waits1, waits2 = {}, {}
-    per = CHUNKS // ROUNDS
 
     def stats_local(r):
-        for n in range(per):
-            d = rows(r * per + n)
-            for k in range(2):
-                peaks = [stat[t, k : k + 1, d] for t in range(tiles)]
-                sums = [stat[t, 2 + k : 3 + k, d] for t in range(tiles)]
-                peak = functools.reduce(jnp.maximum, peaks)
-                total = functools.reduce(jnp.add, [s * jnp.exp2(m - peak) for s, m in zip(sums, peaks)])
-                value = peak + jnp.log(total) * LOG2E
-                for m in range(4):
-                    at = (k * per + n) * 4 + m
-                    sb1[r, at : at + 1, :] = value[:, m * 128 : (m + 1) * 128]
+        n = queries // ROUNDS
+        d = pl.ds(r * n, n)
+        for k in range(2):
+            peak = jnp.max(peaks[k, :, d], axis=0, keepdims=True) * factors[k]
+            value = peak + jnp.log(jnp.sum(totals[k, :, d], axis=0, keepdims=True)) * LOG2E
+            for m in range(n // 128):
+                at = k * (n // 128) + m
+                sb1[r, at : at + 1, :] = value[:, m * 128 : (m + 1) * 128]
         waits1[r] = spread(sb1.at[r], s1.at[r], peers1, lambda n: s1.at[r, n])
 
     def stats_middle(r):
@@ -191,31 +183,35 @@
     def stats_final(r):
         waits2[r].wait_recv()
         lse[r] = log_total([sb2[r]] + [s2[r, n] for n in range(STATS - 1)])
-        for n in range(per):
-            c = r * per + n
-            d = rows(c)
-            lse_s = wide(lse[r, n * 4 : n * 4 + 4, :])
-            lse_t = wide(lse[r, (per + n) * 4 : (per + n) * 4 + 4, :])
-            part = (1.5 * lse_s - lse_t) * (1.0 / 64.0)
-            for t in range(tiles):
-                part = part + stat[t, 4:5, d] * jnp.exp2(stat[t, 1:2, d] - lse_t) - CE_WEIGHT * stat[t, 5:6, d]
-                stat[t, 6:7, d] = (1.0 + CE_WEIGHT) * jnp.exp2(stat[t, 0:1, d] - lse_s)
-                stat[t, 7:8, d] = jnp.exp2(stat[t, 1:2, d] - lse_t)
-            lacc[c : c + 1, :] = part
-
-    def logit_grads(c):
+        n = queries // ROUNDS
+        for k in range(2):
+            lses[k : k + 1, pl.ds(r * n, n)] = wide(lse[r, k * (n // 128) : (k + 1) * (n // 128), :])
+
+    def logit_grads(c, t):
         d = rows(c)
-        positive = pos_ref[0:1, d] - p * passages
-
-        @pl.loop(0, tiles)
-        def _(t):
-            r = pl.ds(pl.multiple_of(t * TILE, TILE), TILE)
-            row = lax.broadcasted_iota(jnp.int32, (TILE, CHUNK), 0) + t * TILE
-            v = es[r, d] * stat[t, 6:7, d] - et[r, d] * stat[t, 7:8, d]
-            g[r, d] = jnp.where(row == positive, v - CE_WEIGHT, v).astype(jnp.bfloat16)
-
-    def query_terms(c):
-        own[rows(c), :] = dot(g[:, rows(c)], sp[...], TN)
+        start = t * TILE if isinstance(t, int) else pl.multiple_of(t * TILE, TILE)
+        r = pl.ds(start, TILE)
+        row = lax.broadcasted_iota(jnp.int32, (TILE, CHUNK), 0)
+        positive = pos_ref[0:1, d] - (p * passages + start)
+        student = jnp.exp2(raw_s[r, d] * cs - (lses[0:1, d] - math.log2(1.0 + CE_WEIGHT)))
+        teacher = jnp.exp2(raw_t[r, d] * ct - lses[1:2, d])
+        v = student - teacher
+        g[r, d] = jnp.where(row == positive, v - CE_WEIGHT, v).astype(jnp.bfloat16)
+
+    def query_terms(c, n):
+        w = ds // 3
+        own[rows(c), n * w : (n + 1) * w] = dot(g[:, rows(c)], sp[:, n * w : (n + 1) * w], TN)
+
+    def loss_terms(i):
+        c, t = divmod(i, tiles)
+        d, r = rows(c), pl.ds(t * TILE, TILE)
+        row = lax.broadcasted_iota(jnp.int32, (TILE, CHUNK), 0)
+        positive = pos_ref[0:1, d] - (p * passages + t * TILE)
+        s2, t2 = raw_s[r, d] * cs, raw_t[r, d] * ct
+        v = jnp.exp2(t2 - lses[1:2, d]) * (t2 - s2)
+        v = jnp.where(row == positive, v - CE_WEIGHT * s2, v)
+        v = jnp.sum(v.reshape(TILE // 8, 8, CHUNK), axis=0)
+        lacc[...] = v if i == 0 else lacc[...] + v
 
     pas_rows = passages // 2
     pas_sent = []
@@ -223,15 +219,18 @@
     def passage_terms(into, first, b, r):
         n, k = TILE, queries // ROUNDS
         at = pl.ds(pl.multiple_of(first + b * n, n), n)
-        term = dot(g[at, pl.ds(r * k, k)], sq[pl.ds(r * k, k), :], NN)
         to = pl.ds(b * n, n)
-        into[to, :] = term if r == 0 else into[to, :] + term
+        if r is None:
+            into[to, :] = dot(g[at, :], sq[...], NN)
+        else:
+            term = dot(g[at, pl.ds(r * k, k)], sq[pl.ds(r * k, k), :], NN)
+            into[to, :] = term if r == 0 else into[to, :] + term
 
     def passage_send(b, r):
         passage_terms(ps, (1 - q) * pas_rows, b, r)
 
-    def passage_own(b, r):
-        passage_terms(pas, q * pas_rows, b, r)
+    def passage_own(b):
+        passage_terms(pas, q * pas_rows, b, None)
 
     def passage_post(n):
         r = pl.ds(sum(PARTS[:n]), PARTS[n])
@@ -320,7 +319,6 @@
                 w[s, 5 + d].wait_recv()
             add(small(s, j), *[near(s, d) for d in range(1, 4)])
             w[s, 9] = post(small(s, j), over(s), across)
-        passage_post(len(pas_sent))
         yield
 
         def place(s, i, j=0, n=piece):
@@ -366,8 +364,13 @@
 
     def loss_sum():
         i1, i2 = core * 4 + y, xh * 4 + z
-        total = jnp.sum(lacc[0:CHUNKS, :], axis=0, keepdims=True)
-        total = functools.reduce(jnp.add, [total[:, n * 128 : (n + 1) * 128] for n in range(CHUNK // 128)])
+        own_share = (1.5 * lses[0:1, :] - lses[1:2, :]) * (1.0 / 64.0)
+        total = jnp.sum(lacc[...], axis=0, keepdims=True)
+        total = functools.reduce(
+            jnp.add,
+            [total[:, n * 128 : (n + 1) * 128] for n in range(CHUNK // 128)]
+            + [own_share[:, n * 128 : (n + 1) * 128] for n in range(queries // 128)],
+        )
         lb1[i1] = jnp.broadcast_to(total, (8, 128))
         wait = spread(lb1.at[i1], lb1, peers1, lambda n: lb1.at[i1])
         yield
@@ -381,61 +384,61 @@
         yield
         last.wait_recv()
         value = jnp.sum(lb3[0, 0:1, :] + lb3[1, 0:1, :], axis=1, keepdims=True) * (LN2 / (2 * queries))
-        loss_ref[...] = jnp.broadcast_to(value, loss_ref.shape)
+        loss_ref[...] = value
         yield
 
     sums = [query_sum(c) for c in range(CHUNKS)]
     loss = loss_sum()
-    for j in range(4):
-        products(0, j)
     logits(0)
-    logits(1)
-    pl.semaphore_wait(barrier, len(everyone))
-    stats_local(0)
-    logits(2)
-    stats_middle(0)
-    logits(3)
+    for u in range(1, units + 1):
+        logits(u)
+        if u == units // 2:
+            pl.semaphore_wait(barrier, len(everyone))
+            stats_local(0)
+        if u == units - 2:
+            stats_middle(0)
     stats_local(1)
     stats_final(0)
-    logit_grads(0)
-    query_terms(0)
+    for t in range(tiles):
+        logit_grads(0, t)
+    for t in range(tiles):
+        if t < 3:
+            query_terms(0, t)
+        logit_grads(1, t)
     next(sums[0])
-    logit_grads(1)
-    query_terms(1)
+    stats_middle(1)
+    for n in range(3):
+        query_terms(1, n)
     next(sums[1])
-    stats_middle(1)
+    passage_send(0, 0)
     next(sums[0])
-    passage_send(0, 0)
     passage_send(1, 0)
-    next(sums[1])
-    passage_own(0, 0)
-    passage_own(1, 0)
-    next(sums[0])
     stats_final(1)
-    logit_grads(2)
-    logit_grads(3)
-    passage_send(0, 1)
-    passage_post(0)
-    passage_send(1, 1)
-    next(sums[1])
-    query_terms(2)
-    next(sums[2])
-    query_terms(3)
-    next(sums[3])
-    next(sums[0])
-    passage_own(0, 1)
-    next(sums[2])
-    passage_own(1, 1)
-    next(sums[1])
-    next(sums[3])
-    stages = {0: 4, 1: 4, 2: 2, 3: 2}
-    for tick in range(4, 20):
-        for c in range(CHUNKS):
-            while stages[c] < 10 and stages[c] + c <= tick:
-                next(sums[c])
-                stages[c] += 1
-        if 7 <= tick < 11:
+    tiles_done, blocks_done = 0, 0
+    for e in EVENTS:
+        if e < 0:
+            passage_post(len(pas_sent))
+        elif e < 4:
+            next(sums[e])
+        elif e == 5:
             next(loss)
+        elif e == 4:
+            for t in range(2):
+                passage_send(t, 1)
+        elif e < 8:
+            c = e - 4
+            for t in range(tiles):
+                logit_grads(c, t)
+            for n in range(3):
+                query_terms(c, n)
+            next(sums[c])
+        elif e == 8:
+            passage_own(blocks_done)
+            blocks_done += 1
+        else:
+            for _ in range(2):
+                loss_terms(tiles_done)
+                tiles_done += 1
     for n in range(len(PARTS)):
         passage_add(n)
     for copy in sent:
@@ -455,8 +458,8 @@
         vmem((passages, dt), bf16),
         vmem((passages, queries), f32),
         vmem((passages, queries), f32),
-        vmem((passages // TILE, 8, queries), f32),
-        *[vmem((TILE, CHUNK), f32), vmem((TILE, CHUNK), f32), vmem((2, 8, CHUNK), f32)] * 2,
+        vmem((2, 8, queries), f32),
+        vmem((2, 8, queries), f32),
         vmem((passages, queries), bf16),
         vmem((queries, ds), f32),
         vmem((queries // 2, ds), f32),
@@ -470,18 +473,19 @@
         vmem((ROUNDS, 16, 128), f32),
         vmem((ROUNDS, STATS - 1, 16, 128), f32),
         vmem((ROUNDS, 16, 128), f32),
+        vmem((8, queries), f32),
         vmem((STATS, 8, 128), f32),
         vmem((STATS, 8, 128), f32),
         vmem((2, 8, 128), f32),
         vmem((8, CHUNK), f32),
         pltpu.SemaphoreType.DMA((180,)),
         pltpu.SemaphoreType.DMA((180,)),
-        pltpu.SemaphoreType.DMA((2 + 2 * CHUNKS,)),
+        pltpu.SemaphoreType.DMA((16,)),
     ]
     loss, query_grads, passage_grads = pl.pallas_call(
         kernel,
         out_shape=(
-            jax.ShapeDtypeStruct((8, 128), f32),
+            jax.ShapeDtypeStruct((1, 1), f32),
             vmem((queries, ds), f32),
             vmem((passages // 2, ds), f32),
         ),
@@ -491,7 +495,7 @@
         compiler_params=pltpu.CompilerParams(collective_id=0, has_side_effects=True, vmem_limit_bytes=52 * 2**20),
         cost_estimate=pl.CostEstimate(flops=14 * 10**9, bytes_accessed=20 * 10**6, transcendentals=4 * 10**6),
     )(student_queries, teacher_queries, student_passages, teacher_passages, positives.reshape(1, queries))
-    return loss[0, 0], query_grads, passage_grads
+    return loss.reshape(()), query_grads, passage_grads
 
 
 def solution(mesh):

time: 91.7 us -> 91.8 us (level)
  between operations: 0.64 us -> 2.33 us
  local copies, waits for them, and re-layouts: 5.03 us -> 3.85 us
    slice x1 -> x0, local copies, waits for them, and re-layouts: 1.18 us -> none  [shards(): return (loss[0, 0], query_grads, passage_grads)]
where the time goes in v3:
time: 91.8 us; the launch traced here: 91.5 us
  Pallas kernels  85.3 us (93%)
  local copies, waits for them, and re-layouts  3.85 us (4%)
  between operations  2.33 us (3%)
    pallas_call x1, Pallas kernels, shards(): pl.pallas_call(kernel, out_shape=(jax.ShapeDtypeStruct((1, 1), f32), vmem...  85.3 us
    unnamed x2, local copies, waits for them, and re-layouts  3.85 us

profile of v3, /device:TPU:1, one launch (start us, length us, event | category | flops | bytes accessed | tf_op | source)
XLA Modules:
  0.0 91.5 jit_solution(13251003563585516973)
XLA Ops:
  0.6 85.3 %shard_map.76 = (f32[1,1]{1,0:T(1,128)}, f32[2048,768]{1,0:T(8,128)S(1)}, f32[512,768]{1,0:T(8,128)S(1)}) custom-call(bf16[2048,768]{1,0:T(8,128)(2,1)} %sq_hbm.1, bf16[2048,1024]{1,0:T(8,128)(2,1)} %tq_hbm.1, bf16[1024,768]{1,0:T(8,128)(2,1)} %sp_hbm.1, bf16[1024,1024]{1,0:T(8,128)(2,1)} %tp_hbm.1, s32[1,2048]{1,0:T(1,128)} %bitcast.2), custom_call_target="tpu_custom_call" | custom-call | flops 14000000000 | bytes 20000000 | tf_op jit(solution)/shard_map/pallas_call | solution.py:485
  86.0 2.7 %copy.11 = f32[2048,768]{1,0:T(8,128)} copy(f32[2048,768]{1,0:T(8,128)S(1)} %get-tuple-element.10) | data formatting | bytes 12582912
  88.7 1.1 %copy.12 = f32[512,768]{1,0:T(8,128)} copy(f32[512,768]{1,0:T(8,128)S(1)} %get-tuple-element.11) | data formatting | bytes 3145728
